TPU v7x, 128 devices: a whole 4x4x4 slice. The times are simulated.
128 devices in a mesh: exp: 8 (over y, z_hi), gy: 4 (over z_lo, core), gz: 4 (over x).
Axes of the slice: x: 4, y: 4, z: 4 (z_hi: 2, z_lo: 2; z = z_hi * 2 + z_lo), core: 2. Of those that a mesh axis runs over, the one named last changes fastest.
Arguments:
- adjoint_final: float32 [8, 128, 128, 1024], P('exp', None, 'gy', 'gz'), may hold values from -6 to 6
- concentration: bfloat16 [2, 8, 128, 128, 1024], P(None, 'exp', None, 'gy', 'gz'), may hold values from 0 to 1
- observed: bfloat16 [2, 8, 128, 128, 1024], P(None, 'exp', None, 'gy', 'gz'), may hold values from 0 to 1
- capacity: float32 [128, 128, 1024], P(None, 'gy', 'gz'), may hold values from 0.03 to 0.3
- pore_mask: int32 [128, 128, 1024], P(None, 'gy', 'gz'), may hold values 0 or 1
- feed_index: int32 [8], P('exp'), may hold values from 0 to 7
- feed_affinity: float32 [8], replicated, may hold values from 0.5 to 4
Outputs:
- adjoint_first: float32 [8, 128, 128, 1024], P('exp', None, 'gy', 'gz')
- capacity_grad: float32 [128, 128, 1024], P('exp', 'gy', 'gz')
All inputs are finite; a program needn't handle non-finite values. No bound on the sum of `pore_mask` on one device may be relied on, other than what follows from the above.
Results may differ from a plain program's by a relative error of at most 0.0003.
Values sent between devices are 32-bit elements; how exact they have to be, the bound alone decides.
No kernel may reach another device: no remote copies, remote signals or barrier semaphores. Data moves between devices by JAX's collectives and lax.ppermute only.
A program may use at most 128 MiB of HBM per device.

v0:
```python
import jax
import jax.numpy as jnp
from jax import lax
from jax.sharding import PartitionSpec as P


def padded(cells, sides, width):
    for axis, dim in sides:
        count = lax.axis_size(axis)
        ends = count - 1
        head = lax.slice_in_dim(cells, 0, width, axis=dim)
        tail = lax.slice_in_dim(cells, cells.shape[dim] - width, cells.shape[dim], axis=dim)
        cells = jnp.concatenate(
            [
                lax.ppermute(tail, axis, [(i, (i + 1) % count) for i in range(ends)]),
                cells,
                lax.ppermute(head, axis, [((i + 1) % count, i) for i in range(ends)]),
            ],
            axis=dim,
        )
    return cells


def face_flux(near_adj, near_pores, adjoint):
    return near_pores * (near_adj - adjoint)


def adjoint_update(adjoint_wide, pores_wide, capacity, affinity, filled_low, observed_low):
    adjoint = adjoint_wide[:, 1:-1, 1:-1]
    pores = pores_wide[:, 1:-1, 1:-1]
    adjoint_x = jnp.pad(adjoint, ((1, 1), (0, 0), (0, 0)))
    pores_x = jnp.pad(pores, ((1, 1), (0, 0), (0, 0)))
    dispersion = face_flux(adjoint_x[2:], pores_x[2:], adjoint) + face_flux(
        adjoint_x[:-2], pores_x[:-2], adjoint
    )
    dispersion = dispersion + face_flux(adjoint_wide[:, 2:, 1:-1], pores_wide[:, 2:, 1:-1], adjoint)
    dispersion = dispersion + face_flux(
        adjoint_wide[:, :-2, 1:-1], pores_wide[:, :-2, 1:-1], adjoint
    )
    dispersion = dispersion + face_flux(adjoint_wide[:, 1:-1, 2:], pores_wide[:, 1:-1, 2:], adjoint)
    dispersion = dispersion + face_flux(
        adjoint_wide[:, 1:-1, :-2], pores_wide[:, 1:-1, :-2], adjoint
    )
    pores_next = jnp.concatenate([pores[1:], jnp.ones_like(pores[:1])], 0)
    adjoint_next = jnp.concatenate([adjoint[1:], jnp.zeros_like(adjoint[:1])], 0)
    transport = pores_next * (adjoint_next - adjoint)
    filled = filled_low.astype(jnp.float32)
    saturation = 1.0 + affinity * filled
    uptake = capacity * affinity / (saturation * saturation)
    updated = pores * (
        adjoint
        + 0.1 * dispersion
        + 0.2 * transport
        - uptake * adjoint
        + (filled - observed_low.astype(jnp.float32))
    )
    gradient_term = -pores * affinity * filled / saturation * adjoint
    return (updated, gradient_term)


def shards(adjoint_final, concentration, observed, capacity, pore_mask, feed_index, feed_affinity):
    pores_wide = padded(pore_mask, (("gy", 1), ("gz", 2)), 1).astype(jnp.float32)
    feeds = jnp.arange(feed_affinity.shape[0], dtype=jnp.int32)
    affinity = jnp.sum(
        jnp.where(feeds == feed_index[0], feed_affinity, jnp.zeros_like(feed_affinity))
    )
    adjoint = adjoint_final[0]
    length = adjoint.shape[0]
    share = length // lax.axis_size("exp")
    gradient = jnp.zeros_like(adjoint)
    for moment in reversed(range(concentration.shape[0])):
        adjoint_wide = padded(adjoint, (("gy", 1), ("gz", 2)), 1)
        adjoint, gradient_term = adjoint_update(
            adjoint_wide,
            pores_wide,
            capacity,
            affinity,
            concentration[moment, 0],
            observed[moment, 0],
        )
        gradient = gradient + gradient_term
    summed = lax.psum(gradient, "exp")
    owned = lax.dynamic_slice_in_dim(summed, lax.axis_index("exp") * share, share, 0)
    return (adjoint[None], owned)


def solution(mesh):
    in_specs = (
        P("exp", None, "gy", "gz"),
        P(None, "exp", None, "gy", "gz"),
        P(None, "exp", None, "gy", "gz"),
        P(None, "gy", "gz"),
        P(None, "gy", "gz"),
        P("exp"),
        P(),
    )
    out_specs = (P("exp", None, "gy", "gz"), P("exp", "gy", "gz"))
    return jax.shard_map(shards, mesh=mesh, in_specs=in_specs, out_specs=out_specs, check_vma=False)
```

profile of v0, /device:TPU:16, one launch (start us, length us, event | category | flops | bytes accessed | tf_op | source)
XLA Modules:
  0.0 328.1 jit_solution(10019507288806775459)
XLA Ops:
  7.2 1.7 fusion.66
  9.0 1.7 collective-permute-start
  10.7 1.3 collective-permute-start.1
  12.0 6.0 %copy.14 = f32[1,128,32,256]{1,2,3,0:T(8,128)} copy(f32[1,128,32,256]{3,2,1,0:T(8,128)} %param.7) | data formatting | bytes 8388608 | tf_op args[0]
  18.0 1.7 fusion.64
  19.8 0.1 copy.15
  19.9 1.3 collective-permute-start.4
  21.2 0.1 copy.17
  21.3 5.6 %collective-permute-start.5 = (f32[128,1,256]{2,0,1:T(8,128)S(1)}, f32[128,1,256]{2,0,1:T(8,128)S(1)}, u32[]{:S(2)}, u32[]{:S(2)}) collective-permute-start(f32[128,1,256]{2,0,1:T(8,128)S(1)} %copy.17), channel_id=1, source_target_pairs={{0,4},{4,8},{8,12},{1,5},{5,9},{9,13},{2,6},{6,10},{10,14},{3,7},{... | collective-permute-start | bytes 393224 | tf_op jit(solution)/shard_map/ppermute | solution.py:15
  26.9 5.3 %slice_bitcast_fusion = f32[127,32,256]{0,1,2:T(8,128)} fusion(f32[1,128,32,256]{1,2,3,0:T(8,128)} %copy.14), kind=kLoop, calls=%fused_computation.72 | loop fusion | bytes 8323072 | tf_op jit(solution)/shard_map/slice | solution.py:45
  32.2 2.6 fusion.65
  34.8 1.1 copy-done.5
  35.9 1.8 fusion.62
  38.3 0.7 fusion.60
  39.0 5.9 %copy.12 = s32[128,32,256]{0,1,2:T(8,128)} copy(s32[128,32,256]{2,1,0:T(8,128)} %param.11) | data formatting | bytes 8388608 | tf_op args[4]
  44.9 5.2 %copy.39 = bf16[1,1,128,32,256]{2,3,4,1,0:T(8,128)(2,1)} copy(bf16[1,1,128,32,256]{4,3,2,1,0:T(8,128)(2,1)} %get-tuple-element.19) | data formatting | bytes 4194304
  50.0 5.2 %copy.37 = bf16[1,1,128,32,256]{2,3,4,1,0:T(8,128)(2,1)} copy(bf16[1,1,128,32,256]{4,3,2,1,0:T(8,128)(2,1)} %get-tuple-element.18) | data formatting | bytes 4194304
  55.2 4.0 %copy.38 = bf16[1,1,128,32,256]{2,3,4,1,0:T(8,128)(2,1)} copy(bf16[1,1,128,32,256]{4,3,2,1,0:T(8,128)(2,1)S(1)} %get-tuple-element.13) | data formatting | bytes 4194304
  59.3 6.0 %copy.22 = f32[128,32,256]{0,1,2:T(8,128)} copy(f32[128,32,256]{2,1,0:T(8,128)} %param.10) | data formatting | bytes 8388608 | tf_op args[3]
  65.3 0.1 copy.13
  65.4 0.8 pad_add_fusion.2
  66.2 3.4 %collective-permute-start.2 = (s32[128,34,1]{0,1,2:T(8,128)S(1)}, s32[128,34,1]{0,1,2:T(8,128)S(1)}, u32[]{:S(2)}, u32[]{:S(2)}) collective-permute-start(s32[128,34,1]{0,1,2:T(8,128)S(1)} %get-tuple-element.10), channel_id=1, source_target_pairs={{0,1},{1,2},{2,3},{4,5},{5,6},{6,7},{8,9},{9,10},{10,11},{12,13},{... | collective-permute-start | bytes 52232 | tf_op jit(solution)/shard_map/ppermute | solution.py:15
  69.6 1.3 collective-permute-start.3
  70.9 0.1 copy.16
  71.1 0.9 pad_maximum_fusion.21
  72.0 1.4 collective-permute-start.6
  73.4 5.4 %collective-permute-start.7 = (f32[128,34,1]{0,1,2:T(8,128)S(1)}, f32[128,34,1]{0,1,2:T(8,128)S(1)}, u32[]{:S(2)}, u32[]{:S(2)}) collective-permute-start(f32[128,34,1]{0,1,2:T(8,128)S(1)} %get-tuple-element.9), channel_id=1, source_target_pairs={{0,1},{1,2},{2,3},{4,5},{5,6},{6,7},{8,9},{9,10},{10,11},{12,13},{... | collective-permute-start | bytes 52232 | tf_op jit(solution)/shard_map/ppermute | solution.py:15
  78.8 1.9 add_convert_fusion
  80.7 3.1 slice.173
  83.8 3.2 slice.180
  87.1 32.2 %fusion.9 = (f32[128,32,256]{0,1,2:T(8,128)}, f32[128,32,256]{0,1,2:T(8,128)}) fusion(bf16[1,1,128,32,256]{2,3,4,1,0:T(8,128)(2,1)} %copy.39, bf16[1,1,128,32,256]{2,3,4,1,0:T(8,128)(2,1)} %copy.37, f32[]{:T(128)} %fusion.60, f32[1,128,32,256]{1,2,3,0:T(8,128)} %copy.14, f32[128,34,258]{0,1,2:T(8,128)S(1)} %add_convert_fusion, f32[128,32,256]{0,1,2:T(8,128)} %slice.173, ...), kind=kLoop, calls=%fused_computation.22 | loop fusion | flops 57671680 | bytes 61048836 | tf_op jit(solution)/shard_map/add | solution.py:81
  119.3 1.7 fusion.63
  121.0 0.1 copy.25
  121.1 1.3 collective-permute-start.8
  122.4 0.1 copy.27
  122.5 3.4 %collective-permute-start.9 = (f32[128,1,256]{2,0,1:T(8,128)S(1)}, f32[128,1,256]{2,0,1:T(8,128)S(1)}, u32[]{:S(2)}, u32[]{:S(2)}) collective-permute-start(f32[128,1,256]{2,0,1:T(8,128)S(1)} %copy.27), channel_id=1, source_target_pairs={{0,4},{4,8},{8,12},{1,5},{5,9},{9,13},{2,6},{6,10},{10,14},{3,7},{... | collective-permute-start | bytes 393224 | tf_op jit(solution)/shard_map/ppermute | solution.py:15
  126.0 0.1 copy.26
  126.1 0.9 collective-permute-done.9
  127.0 0.8 pad_maximum_fusion.18
  127.8 1.3 collective-permute-start.10
  129.1 4.8 %collective-permute-start.11 = (f32[128,34,1]{0,1,2:T(8,128)S(1)}, f32[128,34,1]{0,1,2:T(8,128)S(1)}, u32[]{:S(2)}, u32[]{:S(2)}) collective-permute-start(f32[128,34,1]{0,1,2:T(8,128)S(1)} %get-tuple-element.7), channel_id=1, source_target_pairs={{0,1},{1,2},{2,3},{4,5},{5,6},{6,7},{8,9},{9,10},{10,11},{12,13},{... | collective-permute-start | bytes 52232 | tf_op jit(solution)/shard_map/ppermute | solution.py:15
  133.8 5.3 %copy.40 = bf16[1,1,128,32,256]{2,3,4,1,0:T(8,128)(2,1)} copy(bf16[1,1,128,32,256]{4,3,2,1,0:T(8,128)(2,1)} %get-tuple-element.12) | data formatting | bytes 4194304
  139.2 5.6 %slice.184 = f32[127,32,256]{0,1,2:T(8,128)} slice(f32[128,32,256]{0,1,2:T(8,128)} %get-tuple-element.5), slice={[1:128], [0:32], [0:256]} | slice | bytes 8323072 | tf_op jit(solution)/shard_map/slice | solution.py:45
  144.8 18.8 %fusion.59 = f32[1,128,32,256]{1,2,3,0:T(8,128)} fusion(f32[128,32,256]{0,1,2:T(8,128)} %slice.173, f32[128,32,256]{0,1,2:T(8,128)S(1)} %copy-done.1, f32[127,32,256]{0,1,2:T(8,128)} %slice.184, f32[128,1,256]{0,1,2:T(1,128)S(1)} %copy.26, f32[128,1,256]{0,1,2:T(1,128)S(1)} %copy.28, f32[128,34,1]{0,1,2:T(8,128)S(1)} %collective-permute-done.11, ...), kind=kLoop, calls=%fused_computation.89 | loop fusion | flops 45088768 | bytes 46368772 | tf_op jit(solution)/shard_map/broadcast_in_dim | solution.py:84
  163.7 5.5 %copy.33 = f32[1,128,32,256]{3,2,1,0:T(8,128)} copy(f32[1,128,32,256]{1,2,3,0:T(8,128)} %fusion.59) | data formatting | bytes 8388608
  169.2 142.3 %all-reduce.8.cloned.1.call-done = f32[128,32,256]{0,1,2:T(8,128)} async-done(((f32[128,32,256]{0,1,2:T(8,128)}), f32[128,32,256]{0,1,2:T(8,128)}) %all-reduce.8.cloned.1.call-update) | async-done | bytes 4194320 | tf_op jit(solution)/shard_map/psum | solution.py:82
  311.5 5.3 %constant_dynamic-slice_fusion = f32[16,32,256]{0,1,2:T(8,128)} fusion(f32[128,32,256]{0,1,2:T(8,128)} %all-reduce.8.cloned.1.call-done, s32[]{:T(128)S(6)} %select_n.8), kind=kLoop, calls=%fused_computation.101 | loop fusion | bytes 1048580 | tf_op jit(solution)/shard_map/dynamic_slice | solution.py:83
  316.8 4.5 %copy.34 = f32[16,32,256]{2,1,0:T(8,128)} copy(f32[16,32,256]{0,1,2:T(8,128)} %constant_dynamic-slice_fusion) | data formatting | bytes 1048576
  (36 shorter events, 0.4 us)
Async XLA Ops:
  7.2 304.3 %all-reduce.8.cloned.1.call-start = ((), (), s32[]{:S(2)}) async-start(), calls=%async_computation | async-start | bytes 8388608 | tf_op jit(solution)/shard_map/psum | solution.py:82
  9.0 56.3 %collective-permute-start = (s32[128,1,256]{2,0,1:T(8,128)S(1)}, s32[128,1,256]{2,0,1:T(8,128)S(1)}, u32[]{:S(2)}, u32[]{:S(2)}) collective-permute-start(s32[128,1,256]{2,0,1:T(8,128)S(1)} %copy.35), channel_id=1, source_target_pairs={{0,4},{4,8},{8,12},{1,5},{5,9},{9,13},{2,6},{6,10},{10,14},{3,7},{... | collective-permute-start | bytes 393224 | tf_op jit(solution)/shard_map/ppermute | solution.py:15
  10.7 54.6 %collective-permute-start.1 = (s32[128,1,256]{2,0,1:T(8,128)S(1)}, s32[128,1,256]{2,0,1:T(8,128)S(1)}, u32[]{:S(2)}, u32[]{:S(2)}) collective-permute-start(s32[128,1,256]{2,0,1:T(8,128)S(1)} %copy.36), channel_id=1, source_target_pairs={{4,0},{8,4},{12,8},{5,1},{9,5},{13,9},{6,2},{10,6},{14,10},{7,3},{... | collective-permute-start | bytes 393224 | tf_op jit(solution)/shard_map/ppermute | solution.py:17
  19.9 51.0 %collective-permute-start.4 = (f32[128,1,256]{2,0,1:T(8,128)S(1)}, f32[128,1,256]{2,0,1:T(8,128)S(1)}, u32[]{:S(2)}, u32[]{:S(2)}) collective-permute-start(f32[128,1,256]{2,0,1:T(8,128)S(1)} %copy.15), channel_id=1, source_target_pairs={{4,0},{8,4},{12,8},{5,1},{9,5},{13,9},{6,2},{10,6},{14,10},{7,3},{... | collective-permute-start | bytes 393224 | tf_op jit(solution)/shard_map/ppermute | solution.py:17
  21.3 10.9 %copy-start.4 = (bf16[2,1,128,32,256]{4,3,2,1,0:T(8,128)(2,1)S(1)}, bf16[2,1,128,32,256]{4,3,2,1,0:T(8,128)(2,1)}, u32[]{:S(2)}) copy-start(bf16[2,1,128,32,256]{4,3,2,1,0:T(8,128)(2,1)} %param.8) | copy-start | bytes 12582916
  21.3 49.7 %collective-permute-start.5 = (f32[128,1,256]{2,0,1:T(8,128)S(1)}, f32[128,1,256]{2,0,1:T(8,128)S(1)}, u32[]{:S(2)}, u32[]{:S(2)}) collective-permute-start(f32[128,1,256]{2,0,1:T(8,128)S(1)} %copy.17), channel_id=1, source_target_pairs={{0,4},{4,8},{8,12},{1,5},{5,9},{9,13},{2,6},{6,10},{10,14},{3,7},{... | collective-permute-start | bytes 393224 | tf_op jit(solution)/shard_map/ppermute | solution.py:15
  32.2 3.7 %copy-start.5 = (bf16[2,1,128,32,256]{4,3,2,1,0:T(8,128)(2,1)S(1)}, bf16[2,1,128,32,256]{4,3,2,1,0:T(8,128)(2,1)}, u32[]{:S(2)}) copy-start(bf16[2,1,128,32,256]{4,3,2,1,0:T(8,128)(2,1)} %param.9) | copy-start | bytes 12582916
  35.9 2.4 copy-start.6
  66.2 12.6 %collective-permute-start.2 = (s32[128,34,1]{0,1,2:T(8,128)S(1)}, s32[128,34,1]{0,1,2:T(8,128)S(1)}, u32[]{:S(2)}, u32[]{:S(2)}) collective-permute-start(s32[128,34,1]{0,1,2:T(8,128)S(1)} %get-tuple-element.10), channel_id=1, source_target_pairs={{0,1},{1,2},{2,3},{4,5},{5,6},{6,7},{8,9},{9,10},{10,11},{12,13},{... | collective-permute-start | bytes 52232 | tf_op jit(solution)/shard_map/ppermute | solution.py:15
  69.6 9.2 %collective-permute-start.3 = (s32[128,34,1]{0,1,2:T(8,128)S(1)}, s32[128,34,1]{0,1,2:T(8,128)S(1)}, u32[]{:S(2)}, u32[]{:S(2)}) collective-permute-start(s32[128,34,1]{0,1,2:T(8,128)S(1)} %get-tuple-element.11), channel_id=1, source_target_pairs={{1,0},{2,1},{3,2},{5,4},{6,5},{7,6},{9,8},{10,9},{11,10},{13,12},{... | collective-permute-start | bytes 52232 | tf_op jit(solution)/shard_map/ppermute | solution.py:17
  71.1 7.7 %copy-start.2 = (s32[128,32,256]{0,1,2:T(8,128)S(1)}, s32[128,32,256]{0,1,2:T(8,128)}, u32[]{:S(2)}) copy-start(s32[128,32,256]{0,1,2:T(8,128)} %copy.12) | copy-start | bytes 12582916
  72.0 15.1 %collective-permute-start.6 = (f32[128,34,1]{0,1,2:T(8,128)S(1)}, f32[128,34,1]{0,1,2:T(8,128)S(1)}, u32[]{:S(2)}, u32[]{:S(2)}) collective-permute-start(f32[128,34,1]{0,1,2:T(8,128)S(1)} %get-tuple-element.8), channel_id=1, source_target_pairs={{1,0},{2,1},{3,2},{5,4},{6,5},{7,6},{9,8},{10,9},{11,10},{13,12},{... | collective-permute-start | bytes 52232 | tf_op jit(solution)/shard_map/ppermute | solution.py:17
  73.4 13.7 %collective-permute-start.7 = (f32[128,34,1]{0,1,2:T(8,128)S(1)}, f32[128,34,1]{0,1,2:T(8,128)S(1)}, u32[]{:S(2)}, u32[]{:S(2)}) collective-permute-start(f32[128,34,1]{0,1,2:T(8,128)S(1)} %get-tuple-element.9), channel_id=1, source_target_pairs={{0,1},{1,2},{2,3},{4,5},{5,6},{6,7},{8,9},{9,10},{10,11},{12,13},{... | collective-permute-start | bytes 52232 | tf_op jit(solution)/shard_map/ppermute | solution.py:15
  80.7 6.3 %copy-start = (f32[128,34,258]{0,1,2:T(8,128)}, f32[128,34,258]{0,1,2:T(8,128)S(1)}, u32[]{:S(2)}) copy-start(f32[128,34,258]{0,1,2:T(8,128)S(1)} %add_convert_fusion) | copy-start | bytes 13473796
  121.1 4.8 %collective-permute-start.8 = (f32[128,1,256]{2,0,1:T(8,128)S(1)}, f32[128,1,256]{2,0,1:T(8,128)S(1)}, u32[]{:S(2)}, u32[]{:S(2)}) collective-permute-start(f32[128,1,256]{2,0,1:T(8,128)S(1)} %copy.25), channel_id=1, source_target_pairs={{4,0},{8,4},{12,8},{5,1},{9,5},{13,9},{6,2},{10,6},{14,10},{7,3},{... | collective-permute-start | bytes 393224 | tf_op jit(solution)/shard_map/ppermute | solution.py:17
  122.5 4.4 %collective-permute-start.9 = (f32[128,1,256]{2,0,1:T(8,128)S(1)}, f32[128,1,256]{2,0,1:T(8,128)S(1)}, u32[]{:S(2)}, u32[]{:S(2)}) collective-permute-start(f32[128,1,256]{2,0,1:T(8,128)S(1)} %copy.27), channel_id=1, source_target_pairs={{0,4},{4,8},{8,12},{1,5},{5,9},{9,13},{2,6},{6,10},{10,14},{3,7},{... | collective-permute-start | bytes 393224 | tf_op jit(solution)/shard_map/ppermute | solution.py:15
  127.8 17.0 %collective-permute-start.10 = (f32[128,34,1]{0,1,2:T(8,128)S(1)}, f32[128,34,1]{0,1,2:T(8,128)S(1)}, u32[]{:S(2)}, u32[]{:S(2)}) collective-permute-start(f32[128,34,1]{0,1,2:T(8,128)S(1)} %get-tuple-element.6), channel_id=1, source_target_pairs={{1,0},{2,1},{3,2},{5,4},{6,5},{7,6},{9,8},{10,9},{11,10},{13,12},{... | collective-permute-start | bytes 52232 | tf_op jit(solution)/shard_map/ppermute | solution.py:17
  129.1 15.7 %collective-permute-start.11 = (f32[128,34,1]{0,1,2:T(8,128)S(1)}, f32[128,34,1]{0,1,2:T(8,128)S(1)}, u32[]{:S(2)}, u32[]{:S(2)}) collective-permute-start(f32[128,34,1]{0,1,2:T(8,128)S(1)} %get-tuple-element.7), channel_id=1, source_target_pairs={{0,1},{1,2},{2,3},{4,5},{5,6},{6,7},{8,9},{9,10},{10,11},{12,13},{... | collective-permute-start | bytes 52232 | tf_op jit(solution)/shard_map/ppermute | solution.py:15
  133.8 11.0 %slice-start = ((s8[5283840]{0:T(1024)(128)(4,1)}), s8[1089536]{0:T(1024)(128)(4,1)S(1)}, s32[]{:S(2)}) async-start(s8[5283840]{0:T(1024)(128)(4,1)} %bitcast.24), calls=%async_computation.1 | async-start | bytes 2179072
  133.8 11.0 %copy-start.3 = (bf16[1,1,128,32,256]{2,3,4,1,0:T(8,128)(2,1)S(1)}, bf16[1,1,128,32,256]{2,3,4,1,0:T(8,128)(2,1)}, u32[]{:S(2)}) copy-start(bf16[1,1,128,32,256]{2,3,4,1,0:T(8,128)(2,1)} %copy.39) | copy-start | bytes 6291460
  139.2 5.6 %slice-start.1 = ((s8[5283840]{0:T(1024)(128)(4,1)}), s8[4194304]{0:T(1024)(128)(4,1)S(1)}, s32[]{:S(2)}) async-start(s8[5283840]{0:T(1024)(128)(4,1)} %bitcast.24), calls=%async_computation.2 | async-start | bytes 8388608
  139.2 5.6 %copy-start.1 = (f32[128,32,256]{0,1,2:T(8,128)S(1)}, f32[128,32,256]{0,1,2:T(8,128)}, u32[]{:S(2)}) copy-start(f32[128,32,256]{0,1,2:T(8,128)} %get-tuple-element.5) | copy-start | bytes 12582916
Sparse Core Ops, SparseCore 0:
  119.4 192.0 all-reduce.7
where the time goes:
time: 329 us; the launch traced here: 328 us
  waiting for transfers between devices  143 us (43%)
  local copies, waits for them, and re-layouts  81.7 us (25%)
  other arithmetic  56 us (17%)
  starting transfers between devices  32.2 us (10%)
  between operations  15 us (5%)
    psum x1, waiting for transfers between devices, shards(): summed = lax.psum(gradient, 'exp')  142 us
    unnamed x29, local copies, waits for them, and re-layouts  48.8 us
    add x1, other arithmetic, shards(): gradient = gradient + gradient_term  32.2 us
    ppermute x6, starting transfers between devices, padded(): lax.ppermute(tail, axis, [(i, (i + 1) % count) for i in range(ends)])  24.3 us
    broadcast_in_dim x1, other arithmetic, shards(): return (adjoint[None], owned)  18.8 us
    slice x2, local copies, waits for them, and re-layouts, adjoint_update(): adjoint[1:]  10.9 us
    ppermute x6, starting transfers between devices, padded(): lax.ppermute(head, axis, [((i + 1) % count, i) for i in range(ends)])  7.86 us
  transfers between devices with their start and end apart: 13, of which 2 were waited for; matrix products, arithmetic and copies ran while one was open for 28% of the time, Pallas kernels for 0%

commit v1 on v0

--- a/solution.py
+++ b/solution.py
@@ -79,7 +79,7 @@
             observed[moment, 0],
         )
         gradient = gradient + gradient_term
-    summed = lax.psum(gradient, "exp")
+    summed = jnp.sum(lax.all_gather(gradient, "exp"), axis=0)
     owned = lax.dynamic_slice_in_dim(summed, lax.axis_index("exp") * share, share, 0)
     return (adjoint[None], owned)
 

time: 329 us -> 488 us (1.48)
  waiting for transfers between devices: 143 us -> 285 us
  other arithmetic: 56 us -> 80.5 us
  local copies, waits for them, and re-layouts: 81.7 us -> 72.1 us
    all_gather x0 -> x1, waiting for transfers between devices: none -> 284 us  [shards(): summed = jnp.sum(lax.all_gather(gradient, 'exp'), axis=0)]
    psum x1 -> x0, waiting for transfers between devices: 142 us -> none  [shards(): summed = lax.psum(gradient, 'exp')]
    reduce_sum x0 -> x1, other arithmetic: none -> 14.7 us  [shards(): summed = jnp.sum(lax.all_gather(gradient, 'exp'), axis=0)]
    broadcast_in_dim x1, other arithmetic: 18.8 us -> 28.6 us  [shards(): return (adjoint[None], owned)]
    unnamed x29 -> x26, local copies, waits for them, and re-layouts: 48.8 us -> 41.1 us
    add x0 -> x1, local copies, waits for them, and re-layouts: none -> 5.47 us  [shards(): gradient = gradient + gradient_term]
  transfers between devices with their start and end apart: 13 -> 13, of which waited for: 2 -> 2; matrix products, arithmetic and copies ran while one was open for 28% -> 18% of each run, Pallas kernels for 0% -> 0%
where the time goes in v1:
time: 488 us; the launch traced here: 484 us
  waiting for transfers between devices  285 us (58%)
  other arithmetic  80.5 us (16%)
  local copies, waits for them, and re-layouts  72.1 us (15%)
  starting transfers between devices  32.2 us (7%)
  between operations  14.9 us (3%)
    all_gather x1, waiting for transfers between devices, shards(): summed = jnp.sum(lax.all_gather(gradient, 'exp'), axis=0)  284 us
    unnamed x26, local copies, waits for them, and re-layouts  41.1 us
    add x1, other arithmetic, shards(): gradient = gradient + gradient_term  33.9 us
    broadcast_in_dim x1, other arithmetic, shards(): return (adjoint[None], owned)  28.6 us
    ppermute x6, starting transfers between devices, padded(): lax.ppermute(tail, axis, [(i, (i + 1) % count) for i in range(ends)])  24.4 us
    reduce_sum x1, other arithmetic, shards(): summed = jnp.sum(lax.all_gather(gradient, 'exp'), axis=0)  14.7 us
  transfers between devices with their start and end apart: 13, of which 2 were waited for; matrix products, arithmetic and copies ran while one was open for 18% of the time, Pallas kernels for 0%

profile of v1, /device:TPU:16, one launch (start us, length us, event | category | flops | bytes accessed | tf_op | source)
XLA Modules:
  0.0 484.4 jit_solution(11535588039760264501)
XLA Ops:
  7.2 0.0 all-gather.3.cloned.1.call-start
  7.2 5.3 %copy.9 = s32[128,32,256]{0,2,1:T(8,128)} copy(s32[128,32,256]{2,1,0:T(8,128)} %param.11) | data formatting | bytes 8388608 | tf_op args[4]
  12.5 1.0 fusion.66
  13.5 1.7 collective-permute-start
  15.2 1.3 collective-permute-start.1
  16.5 5.4 %copy.12 = f32[1,128,32,256]{1,3,2,0:T(8,128)} copy(f32[1,128,32,256]{3,2,1,0:T(8,128)} %param.7) | data formatting | bytes 8388608 | tf_op args[0]
  22.0 1.0 fusion.64
  22.9 1.3 collective-permute-start.4
  24.2 0.0 copy-start.4
  24.3 5.6 %collective-permute-start.5 = (f32[128,1,256]{0,2,1:T(8,128)S(1)}, f32[128,1,256]{0,2,1:T(8,128)S(1)}, u32[]{:S(2)}, u32[]{:S(2)}) collective-permute-start(f32[128,1,256]{0,2,1:T(8,128)S(1)} %get-tuple-element.16), channel_id=1, source_target_pairs={{0,4},{4,8},{8,12},{1,5},{5,9},{9,13},{2,6},{6,10},{10,14},{3,7},{... | collective-permute-start | bytes 393224 | tf_op jit(solution)/shard_map/ppermute | solution.py:15
  29.9 5.3 %slice_bitcast_fusion = f32[127,32,256]{0,2,1:T(8,128)} fusion(f32[1,128,32,256]{1,3,2,0:T(8,128)} %copy.12), kind=kLoop, calls=%fused_computation.72 | loop fusion | bytes 8323072 | tf_op jit(solution)/shard_map/slice | solution.py:45
  35.2 2.6 fusion.65
  37.8 1.1 copy-done.5
  38.9 2.5 fusion.62
  42.0 0.7 fusion.60
  42.7 3.4 copy.23
  46.2 4.6 copy.21
  50.7 4.5 copy.22
  55.2 5.3 %copy.14 = f32[128,32,256]{0,2,1:T(8,128)} copy(f32[128,32,256]{2,1,0:T(8,128)} %param.10) | data formatting | bytes 8388608 | tf_op args[3]
  60.6 0.0 collective-permute-done
  60.6 0.0 collective-permute-done.1
  60.6 1.1 pad_add_fusion.2
  61.7 3.7 collective-permute-start.2
  65.4 1.3 collective-permute-start.3
  66.8 1.3 collective-permute-start.6
  68.1 5.2 %collective-permute-start.7 = (f32[128,34,1]{0,2,1:T(1,128)S(1)}, f32[128,34,1]{0,2,1:T(1,128)S(1)}, u32[]{:S(2)}, u32[]{:S(2)}) collective-permute-start(f32[128,34,1]{0,2,1:T(1,128)S(1)} %get-tuple-element.9), channel_id=1, source_target_pairs={{0,1},{1,2},{2,3},{4,5},{5,6},{6,7},{8,9},{9,10},{10,11},{12,13},{... | collective-permute-start | bytes 52232 | tf_op jit(solution)/shard_map/ppermute | solution.py:15
  73.3 0.5 add_convert_fusion
  73.8 2.8 slice.175
  76.6 3.2 slice.182
  79.8 33.9 %fusion.9 = (f32[128,32,256]{0,2,1:T(8,128)}, f32[128,32,256]{0,2,1:T(8,128)}) fusion(bf16[1,1,128,32,256]{2,4,3,1,0:T(8,128)(2,1)S(1)} %copy.23, bf16[1,1,128,32,256]{2,4,3,1,0:T(8,128)(2,1)} %copy.21, f32[]{:T(128)} %fusion.60, f32[1,128,32,256]{1,3,2,0:T(8,128)} %copy.12, f32[128,34,258]{0,2,1:T(8,128)S(1)} %add_convert_fusion, ...), kind=kLoop, calls=%fused_computation.22 | loop fusion | flops 57671680 | bytes 61048836 | tf_op jit(solution)/shard_map/add | solution.py:81
  113.7 5.5 %copy.19 = f32[128,32,256]{2,1,0:T(8,128)} copy(f32[128,32,256]{0,2,1:T(8,128)} %get-tuple-element.4) | data formatting | bytes 8388608 | tf_op jit(solution)/shard_map/add | solution.py:81
  119.2 0.0 all-gather.3.cloned.1.call-update
  119.2 1.0 fusion.63
  120.2 1.3 collective-permute-start.8
  121.5 3.4 collective-permute-start.9
  124.9 1.0 collective-permute-done.9
  125.9 1.0 pad_maximum_fusion.18
  126.9 1.3 collective-permute-start.10
  128.2 4.7 collective-permute-start.11
  132.9 4.7 copy.24
  137.7 4.3 slice.186
  142.0 0.6 slice-done.1
  142.6 0.7 copy-done.3
  143.3 28.6 %fusion.59 = f32[1,128,32,256]{1,3,2,0:T(8,128)} fusion(f32[128,32,256]{0,2,1:T(8,128)} %slice.175, f32[128,32,256]{0,2,1:T(8,128)} %get-tuple-element.5, f32[127,32,256]{0,2,1:T(8,128)S(1)} %slice.186, f32[128,1,256]{0,2,1:T(8,128)S(1)} %collective-permute-done.8, f32[128,1,256]{0,2,1:T(8,128)S(1)} %collective-permute-done.9, ...), kind=kLoop, calls=%fused_computation.89 | loop fusion | flops 45088768 | bytes 46368772 | tf_op jit(solution)/shard_map/broadcast_in_dim | solution.py:84
  171.8 5.4 %copy.20 = f32[1,128,32,256]{3,2,1,0:T(8,128)} copy(f32[1,128,32,256]{1,3,2,0:T(8,128)} %fusion.59) | data formatting | bytes 8388608
  177.3 283.6 %all-gather.3.cloned.1.call-done = f32[1024,32,256]{2,1,0:T(8,128)} async-done(((f32[128,32,256]{2,1,0:T(8,128)}), f32[1024,32,256]{2,1,0:T(8,128)}) %all-gather.3.cloned.1.call-update) | async-done | bytes 33554448 | tf_op jit(solution)/shard_map/all_gather | solution.py:82
  460.9 14.7 %reduce_sum.19 = f32[128,32,256]{2,1,0:T(8,128)} reduce(f32[8,128,32,256]{3,2,1,0:T(8,128)} %bitcast.30, f32[]{:T(128)} %constant.9.clone.1), dimensions={0}, to_apply=%region_1.2 | reduce | flops 7340032 | bytes 37748740 | tf_op jit(solution)/shard_map/reduce_sum | solution.py:82
  475.6 1.9 constant_dynamic-slice_fusion
  (25 shorter events, 0.1 us)
Async XLA Ops:
  7.2 453.7 %all-gather.3.cloned.1.call-start = ((), (), s32[]{:S(2)}) async-start(), calls=%async_computation | async-start | bytes 37748736 | tf_op jit(solution)/shard_map/all_gather | solution.py:82
  13.5 47.1 %collective-permute-start = (s32[128,1,256]{0,2,1:T(8,128)S(1)}, s32[128,1,256]{0,2,1:T(8,128)S(1)}, u32[]{:S(2)}, u32[]{:S(2)}) collective-permute-start(s32[128,1,256]{0,2,1:T(8,128)S(1)} %get-tuple-element.20), channel_id=1, source_target_pairs={{0,4},{4,8},{8,12},{1,5},{5,9},{9,13},{2,6},{6,10},{10,14},{3,7},{... | collective-permute-start | bytes 393224 | tf_op jit(solution)/shard_map/ppermute | solution.py:15
  15.2 45.3 %collective-permute-start.1 = (s32[128,1,256]{0,2,1:T(8,128)S(1)}, s32[128,1,256]{0,2,1:T(8,128)S(1)}, u32[]{:S(2)}, u32[]{:S(2)}) collective-permute-start(s32[128,1,256]{0,2,1:T(8,128)S(1)} %get-tuple-element.21), channel_id=1, source_target_pairs={{4,0},{8,4},{12,8},{5,1},{9,5},{13,9},{6,2},{10,6},{14,10},{7,3},{... | collective-permute-start | bytes 393224 | tf_op jit(solution)/shard_map/ppermute | solution.py:17
  22.9 43.7 %collective-permute-start.4 = (f32[128,1,256]{0,2,1:T(8,128)S(1)}, f32[128,1,256]{0,2,1:T(8,128)S(1)}, u32[]{:S(2)}, u32[]{:S(2)}) collective-permute-start(f32[128,1,256]{0,2,1:T(8,128)S(1)} %get-tuple-element.17), channel_id=1, source_target_pairs={{4,0},{8,4},{12,8},{5,1},{9,5},{13,9},{6,2},{10,6},{14,10},{7,3},{... | collective-permute-start | bytes 393224 | tf_op jit(solution)/shard_map/ppermute | solution.py:17
  24.2 10.9 %copy-start.4 = (bf16[2,1,128,32,256]{4,3,2,1,0:T(8,128)(2,1)S(1)}, bf16[2,1,128,32,256]{4,3,2,1,0:T(8,128)(2,1)}, u32[]{:S(2)}) copy-start(bf16[2,1,128,32,256]{4,3,2,1,0:T(8,128)(2,1)} %param.8) | copy-start | bytes 12582916
  24.3 42.4 %collective-permute-start.5 = (f32[128,1,256]{0,2,1:T(8,128)S(1)}, f32[128,1,256]{0,2,1:T(8,128)S(1)}, u32[]{:S(2)}, u32[]{:S(2)}) collective-permute-start(f32[128,1,256]{0,2,1:T(8,128)S(1)} %get-tuple-element.16), channel_id=1, source_target_pairs={{0,4},{4,8},{8,12},{1,5},{5,9},{9,13},{2,6},{6,10},{10,14},{3,7},{... | collective-permute-start | bytes 393224 | tf_op jit(solution)/shard_map/ppermute | solution.py:15
  35.2 3.7 copy-start.5
  38.9 3.1 copy-start.6
  60.6 6.2 %copy-start.1 = (f32[1,128,32,256]{1,3,2,0:T(8,128)S(1)}, f32[1,128,32,256]{1,3,2,0:T(8,128)}, u32[]{:S(2)}) copy-start(f32[1,128,32,256]{1,3,2,0:T(8,128)} %copy.12) | copy-start | bytes 12582916
  60.6 12.7 %copy-start.2 = (s32[128,32,256]{0,2,1:T(8,128)S(1)}, s32[128,32,256]{0,2,1:T(8,128)}, u32[]{:S(2)}) copy-start(s32[128,32,256]{0,2,1:T(8,128)} %copy.9) | copy-start | bytes 12582916
  61.7 11.5 %collective-permute-start.2 = (s32[128,34,1]{0,2,1:T(1,128)S(1)}, s32[128,34,1]{0,2,1:T(1,128)S(1)}, u32[]{:S(2)}, u32[]{:S(2)}) collective-permute-start(s32[128,34,1]{0,2,1:T(1,128)S(1)} %get-tuple-element.10), channel_id=1, source_target_pairs={{0,1},{1,2},{2,3},{4,5},{5,6},{6,7},{8,9},{9,10},{10,11},{12,13},{... | collective-permute-start | bytes 52232 | tf_op jit(solution)/shard_map/ppermute | solution.py:15
  65.4 7.9 %collective-permute-start.3 = (s32[128,34,1]{0,2,1:T(1,128)S(1)}, s32[128,34,1]{0,2,1:T(1,128)S(1)}, u32[]{:S(2)}, u32[]{:S(2)}) collective-permute-start(s32[128,34,1]{0,2,1:T(1,128)S(1)} %get-tuple-element.11), channel_id=1, source_target_pairs={{1,0},{2,1},{3,2},{5,4},{6,5},{7,6},{9,8},{10,9},{11,10},{13,12},{... | collective-permute-start | bytes 52232 | tf_op jit(solution)/shard_map/ppermute | solution.py:17
  66.8 13.0 %collective-permute-start.6 = (f32[128,34,1]{0,2,1:T(1,128)S(1)}, f32[128,34,1]{0,2,1:T(1,128)S(1)}, u32[]{:S(2)}, u32[]{:S(2)}) collective-permute-start(f32[128,34,1]{0,2,1:T(1,128)S(1)} %get-tuple-element.8), channel_id=1, source_target_pairs={{1,0},{2,1},{3,2},{5,4},{6,5},{7,6},{9,8},{10,9},{11,10},{13,12},{... | collective-permute-start | bytes 52232 | tf_op jit(solution)/shard_map/ppermute | solution.py:17
  68.1 11.7 %collective-permute-start.7 = (f32[128,34,1]{0,2,1:T(1,128)S(1)}, f32[128,34,1]{0,2,1:T(1,128)S(1)}, u32[]{:S(2)}, u32[]{:S(2)}) collective-permute-start(f32[128,34,1]{0,2,1:T(1,128)S(1)} %get-tuple-element.9), channel_id=1, source_target_pairs={{0,1},{1,2},{2,3},{4,5},{5,6},{6,7},{8,9},{9,10},{10,11},{12,13},{... | collective-permute-start | bytes 52232 | tf_op jit(solution)/shard_map/ppermute | solution.py:15
  73.8 6.0 %copy-start = (f32[128,34,258]{0,2,1:T(8,128)}, f32[128,34,258]{0,2,1:T(8,128)S(1)}, u32[]{:S(2)}) copy-start(f32[128,34,258]{0,2,1:T(8,128)S(1)} %add_convert_fusion) | copy-start | bytes 13473796
  120.2 4.7 collective-permute-start.8
  121.5 4.4 collective-permute-start.9
  126.9 15.1 %collective-permute-start.10 = (f32[128,34,1]{0,2,1:T(1,128)S(1)}, f32[128,34,1]{0,2,1:T(1,128)S(1)}, u32[]{:S(2)}, u32[]{:S(2)}) collective-permute-start(f32[128,34,1]{0,2,1:T(1,128)S(1)} %get-tuple-element.6), channel_id=1, source_target_pairs={{1,0},{2,1},{3,2},{5,4},{6,5},{7,6},{9,8},{10,9},{11,10},{13,12},{... | collective-permute-start | bytes 52232 | tf_op jit(solution)/shard_map/ppermute | solution.py:17
  128.2 13.8 %collective-permute-start.11 = (f32[128,34,1]{0,2,1:T(1,128)S(1)}, f32[128,34,1]{0,2,1:T(1,128)S(1)}, u32[]{:S(2)}, u32[]{:S(2)}) collective-permute-start(f32[128,34,1]{0,2,1:T(1,128)S(1)} %get-tuple-element.7), channel_id=1, source_target_pairs={{0,1},{1,2},{2,3},{4,5},{5,6},{6,7},{8,9},{9,10},{10,11},{12,13},{... | collective-permute-start | bytes 52232 | tf_op jit(solution)/shard_map/ppermute | solution.py:15
  137.7 4.3 slice-start
  137.7 4.9 %slice-start.1 = ((s8[4595712]{0:T(1024)(128)(4,1)}), s8[4194304]{0:T(1024)(128)(4,1)S(1)}, s32[]{:S(2)}) async-start(s8[4595712]{0:T(1024)(128)(4,1)} %bitcast.25), calls=%async_computation.2 | async-start | bytes 8388608
  137.7 5.6 %copy-start.3 = (bf16[1,1,128,32,256]{2,4,3,1,0:T(8,128)(2,1)S(1)}, bf16[1,1,128,32,256]{2,4,3,1,0:T(8,128)(2,1)}, u32[]{:S(2)}) copy-start(bf16[1,1,128,32,256]{2,4,3,1,0:T(8,128)(2,1)} %copy.24) | copy-start | bytes 6291460
Sparse Core Ops, SparseCore 0:
  119.3 341.5 all-gather.2
